TPU v7x, 32 devices: a whole 2x2x4 slice. The times are simulated.
32 devices in a mesh: row: 4 (over y, core), col: 8 (over z, x).
Axes of the slice: x: 2, y: 2, z: 4, core: 2. Of those that a mesh axis runs over, the one named last changes fastest.
Arguments:
- features: float32 [4096, 1536], P('row', 'col'), may hold values from -6 to 6
Outputs:
- panel: float32 [4096, 512], P('row')
- trailing: float32 [4096, 4096], P('row', 'col')
All inputs are finite; a program needn't handle non-finite values.
Results may differ from a plain program's by a relative error of at most 0.0003.
Values sent between devices are 32-bit elements; how exact they have to be, the bound alone decides.
A program may use at most 64 MiB of HBM per device.

v0:
```python
import jax
import jax.numpy as jnp
from jax import lax
from jax.sharding import PartitionSpec as P

D = 1536


gamma_scale = 0.6
ridge_value = 0.05


def spread(value, axis, source):
    kept = jnp.where(lax.axis_index(axis) == source, value, 0).astype(value.dtype)
    return lax.psum(kept, axis)


def gauss_tile(left_rows, right_rows, row_start, col_start):
    left_sq = jnp.sum(left_rows * left_rows, axis=1)
    right_sq = jnp.sum(right_rows * right_rows, axis=1)
    inner_prod = jnp.dot(
        left_rows, right_rows.T, precision=lax.Precision.HIGHEST, preferred_element_type=jnp.float32
    )
    distance = left_sq[:, None] + right_sq[None, :] - 2.0 * inner_prod
    kernel_value = jnp.exp(-distance * (gamma_scale / D))
    row_index = row_start + jnp.arange(left_rows.shape[0], dtype=jnp.int32)
    col_index = col_start + jnp.arange(right_rows.shape[0], dtype=jnp.int32)
    return kernel_value + jnp.where(
        row_index[:, None] == col_index[None, :], ridge_value, 0.0
    ).astype(jnp.float32)


def solve_rows(some_rows, head_rows, first_index, inverse):
    side_tile = gauss_tile(some_rows, head_rows, first_index, 0)
    return jnp.dot(
        side_tile, inverse.T, precision=lax.Precision.HIGHEST, preferred_element_type=jnp.float32
    )


def on_device(features):
    row_count = lax.axis_size("row")
    col_count = lax.axis_size("col")
    row_id = lax.axis_index("row")
    col_id = lax.axis_index("col")
    row_feat = lax.all_gather(features, "col", axis=1, tiled=True)
    row_height = row_feat.shape[0]
    col_ratio = col_count // row_count
    panel_width = row_height // col_ratio
    row_offset = col_id % col_ratio * panel_width
    owner_row = col_id // col_ratio
    col_feat = spread(
        lax.dynamic_slice_in_dim(row_feat, row_offset, panel_width, 0), "row", owner_row
    )
    head_part = spread(features[:panel_width], "row", 0)
    head_rows = lax.all_gather(head_part, "col", axis=1, tiled=True)
    corner = gauss_tile(head_rows, head_rows, 0, 0)
    chol_factor = jnp.linalg.cholesky(corner)
    inverse = lax.linalg.triangular_solve(
        chol_factor, jnp.eye(panel_width, dtype=jnp.float32), left_side=True, lower=True
    )
    row_start = row_id * row_height
    col_start = col_id * panel_width
    kernel_tile = gauss_tile(row_feat, col_feat, row_start, col_start)
    row_piece = row_height // col_count
    piece_rows = lax.dynamic_slice_in_dim(row_feat, col_id * row_piece, row_piece, 0)
    piece_solved = solve_rows(piece_rows, head_rows, row_start + col_id * row_piece, inverse)
    solved_rows = lax.all_gather(piece_solved, "col", axis=0, tiled=True)
    positions = row_start + jnp.arange(row_height, dtype=jnp.int32)
    top_rows = jnp.concatenate(
        [chol_factor, jnp.zeros((row_height - panel_width, panel_width), jnp.float32)], axis=0
    )
    panel_out = jnp.where(positions[:, None] < panel_width, top_rows, solved_rows)
    masked = jnp.where(positions[:, None] < panel_width, 0.0, solved_rows)
    far_panel = solve_rows(col_feat, head_rows, col_start, inverse)
    col_positions = col_start + jnp.arange(panel_width, dtype=jnp.int32)
    far_panel = jnp.where(col_positions[:, None] < panel_width, 0.0, far_panel)
    trailing = kernel_tile - jnp.dot(
        masked, far_panel.T, precision=lax.Precision.HIGHEST, preferred_element_type=jnp.float32
    )
    return (panel_out, trailing)


def solution(mesh):
    return jax.shard_map(
        on_device,
        mesh=mesh,
        in_specs=(P("row", "col"),),
        out_specs=(P("row", None), P("row", "col")),
        check_vma=False,
    )
```

profile of v0, /device:TPU:0, one launch (start us, length us, event | category | flops | bytes accessed | tf_op | source)
XLA Modules:
  0.0 512.9 jit_solution(6043388997813852830)
XLA Ops:
  8.0 1.8 slice_select_fusion
  9.7 102.2 %all-gather.6.cloned.1.call-done = f32[1024,1536]{0,1:T(8,128)} async-done(((f32[1024,192]{0,1:T(8,128)}), f32[1024,1536]{0,1:T(8,128)}) %all-gather.6.cloned.1.call-update) | async-done | bytes 6291472 | tf_op jit(solution)/shard_map/all_gather | solution.py:45
  111.9 3.9 dynamic-slice_select_fusion
  115.9 73.3 %all-reduce.5.cloned.1.call-done = (f32[512,192]{0,1:T(8,128)}, f32[512,1536]{0,1:T(8,128)}) async-done(((f32[512,192]{0,1:T(8,128)}, f32[512,1536]{0,1:T(8,128)}), (f32[512,192]{0,1:T(8,128)}, f32[512,1536]{0,1:T(8,128)})) %all-reduce.5.cloned.1.call-update) | async-done | bytes 3538960 | tf_op jit(solution)/shard_map/psum | solution.py:15
  190.1 1.2 fusion.34
  191.3 1.3 multiply_reduce_fusion.3
  192.6 59.4 %all-gather.4.cloned.1.call-done = f32[512,1536]{0,1:T(8,128)} async-done(((f32[512,192]{0,1:T(8,128)}), f32[512,1536]{0,1:T(8,128)}) %all-gather.4.cloned.1.call-update) | async-done | bytes 3145744 | tf_op jit(solution)/shard_map/all_gather | solution.py:55
  252.0 2.3 multiply_reduce_fusion.2
  254.8 7.0 %broadcast_add_fusion = (f32[512,512]{0,1:T(8,128)}, f32[512,512]{0,1:T(8,128)}, f32[512,512]{0,1:T(8,128)}) fusion(f32[512]{0:T(512)S(1)} %multiply_reduce_fusion.2, f32[512,1536]{0,1:T(8,128)S(1)} %copy-done), kind=kOutput, calls=%fused_computation.71 | convolution fusion | flops 4833935360 | bytes 6293504 | tf_op jit(solution)/shard_map/dot_general | solution.py:21
  261.8 2.5 copy.6
  264.4 2.5 copy.8
  266.9 2.2 fusion.19
  270.1 11.7 %cholesky.103 = f32[128,128]{1,0:T(8,128)S(1)} custom-call(f32[128,128]{1,0:T(8,128)S(1)} %cholesky.263), custom_call_target="Cholesky" | custom-call | tf_op jit(solution)/shard_map/jit(cholesky)/cholesky | solution.py:57
  281.9 1.1 cholesky.222
  283.0 10.0 %custom-call.30 = f32[1,128,128]{1,2,0:T(8,128)S(1)} custom-call(f32[1,128,128]{2,1,0:T(8,128)S(1)} %get-tuple-element.33), custom_call_target="InvertDiagBlocksLowerTriangular" | custom-call | tf_op jit(solution)/shard_map/jit(cholesky)/cholesky | solution.py:57
  292.9 1.9 constant_dynamic-update-slice_fusion.3
  294.9 1.2 convolution_subtract_fusion.3
  296.1 11.7 %cholesky.215 = f32[128,128]{1,0:T(8,128)S(1)} custom-call(f32[128,128]{1,0:T(8,128)S(1)} %cholesky.267), custom_call_target="Cholesky" | custom-call | tf_op jit(solution)/shard_map/jit(cholesky)/cholesky | solution.py:57
  308.5 9.8 %custom-call.31 = f32[1,128,128]{1,2,0:T(8,128)S(1)} custom-call(f32[1,128,128]{2,1,0:T(8,128)S(1)} %get-tuple-element.30), custom_call_target="InvertDiagBlocksLowerTriangular" | custom-call | tf_op jit(solution)/shard_map/jit(cholesky)/cholesky | solution.py:57
  319.2 1.4 convolution_subtract_fusion.4
  320.7 12.1 %cholesky.236 = f32[128,128]{1,0:T(8,128)S(1)} custom-call(f32[128,128]{1,0:T(8,128)S(1)} %cholesky.272), custom_call_target="Cholesky" | custom-call | tf_op jit(solution)/shard_map/jit(cholesky)/cholesky | solution.py:57
  334.0 9.8 %custom-call.32 = f32[1,128,128]{1,2,0:T(8,128)S(1)} custom-call(f32[1,128,128]{2,1,0:T(8,128)S(1)} %get-tuple-element.27), custom_call_target="InvertDiagBlocksLowerTriangular" | custom-call | tf_op jit(solution)/shard_map/jit(cholesky)/cholesky | solution.py:57
  344.7 1.4 convolution_subtract_fusion.5
  346.1 11.7 %cholesky.253 = f32[128,128]{1,0:T(8,128)S(1)} custom-call(f32[128,128]{1,0:T(8,128)S(1)} %convolution_subtract_fusion.5), custom_call_target="Cholesky" | custom-call | tf_op jit(solution)/shard_map/jit(cholesky)/cholesky | solution.py:57
  362.1 2.8 fusion.25
  364.9 13.4 %while.1 = (s32[]{:T(128)}, f32[512,512]{1,0:T(8,128)}, s32[4,2]{0,1:T(2,128)S(1)}, f32[4,128,128]{2,1,0:T(8,128)}, s32[]{:T(128)}) while((s32[]{:T(128)}, f32[512,512]{1,0:T(8,128)}, s32[4,2]{0,1:T(2,128)S(1)}, f32[4,128,128]{2,1,0:T(8,128)}, s32[]{:T(128)}) %tuple.34), condition=%wide.while_cond, body=%wide.while_body.sunk | while | flops 2 | bytes 132705 | solution.py:58
  365.5 2.8 bitcast_dynamic-update-slice_fusion.2
  368.8 2.8 bitcast_dynamic-update-slice_fusion.2
  372.2 2.8 bitcast_dynamic-update-slice_fusion.2
  375.5 2.7 bitcast_dynamic-update-slice_fusion.2
  378.2 40.9 %custom-call.33 = f32[4,128,128]{1,2,0:T(8,128)} custom-call(f32[4,128,128]{2,1,0:T(8,128)} %get-tuple-element.9), custom_call_target="InvertDiagBlocksLowerTriangular" | custom-call | tf_op jit(solution)/shard_map/triangular_solve | solution.py:58
  419.1 1.2 fusion.43
  420.3 1.6 convolution_subtract_fusion.1
  421.9 1.3 fusion.55
  423.2 2.1 convolution_subtract_fusion
  425.3 1.3 fusion.53
  426.6 2.6 convolution_subtract_fusion.2
  429.2 1.3 fusion.52
  430.5 3.3 fusion.13
  433.8 1.9 fusion.33
  435.7 3.4 multiply_reduce_fusion
  439.7 6.4 %fusion.8 = f32[512,512]{0,1:T(8,128)} fusion(f32[512,1536]{0,1:T(8,128)S(1)} %copy-done.3, f32[512,1536]{0,1:T(8,128)S(1)} %copy-done, f32[512]{0:T(512)S(1)} %multiply_reduce_fusion.1, f32[512]{0:T(512)S(1)} %multiply_reduce_fusion.2), kind=kOutput, calls=%fused_computation.19 | convolution fusion | flops 4832886784 | bytes 7344128 | tf_op jit(solution)/shard_map/dot_general | solution.py:21
  446.2 1.6 copy.10
  447.7 3.2 convolution_select_fusion
  450.9 32.8 %all-gather.8.cloned.1.call-done = f32[1024,512]{1,0:T(8,128)} async-done(((f32[128,512]{1,0:T(8,128)}), f32[1024,512]{1,0:T(8,128)}) %all-gather.8.cloned.1.call-update) | async-done | bytes 2097168 | tf_op jit(solution)/shard_map/all_gather | solution.py:67
  483.8 5.3 %fusion.5 = f32[1024,512]{1,0:T(8,128)S(1)} fusion(f32[512,512]{1,0:T(8,128)S(1)} %convolution_select_fusion, f32[1024,512]{1,0:T(8,128)} %all-gather.8.cloned.1.call-done, pred[1024]{0:T(1024)(128)(4,1)S(1)} %broadcast_compare_fusion), kind=kOutput, calls=%fused_computation.12 | convolution fusion | flops 3221749760 | bytes 5243904 | tf_op jit(solution)/shard_map/dot_general | solution.py:77
  489.1 1.6 pad_select_fusion
  491.7 14.2 %fusion.4 = f32[1024,512]{1,0:T(8,128)} fusion(f32[1024,512]{1,0:T(8,128)S(1)} %fusion.5, f32[512,1536]{0,1:T(8,128)S(1)} %copy-done.4, f32[1024,1536]{0,1:T(8,128)} %all-gather.6.cloned.1.call-done, s32[512]{0:T(512)S(1)} %iota_add_fusion.1, f32[512]{0:T(512)S(1)} %multiply_reduce_fusion.1, f32[1024]{0:T(1024)S(1)} %multiply_reduce_fusion, ...), kind=kOutput, calls=%fused_computation.11 | convolution fusion | flops 9668395008 | bytes 13643776 | tf_op jit(solution)/shard_map/dot_general | solution.py:21
  (56 shorter events, 12.8 us)
Async XLA Ops:
  7.2 104.8 %all-gather.6.cloned.1.call-start = ((), (), s32[]{:S(2)}) async-start(), calls=%async_computation.1 | async-start | bytes 7077888 | tf_op jit(solution)/shard_map/all_gather | solution.py:45
  7.9 181.3 %all-reduce.5.cloned.1.call-start = ((), (), s32[]{:S(2)}) async-start(), calls=%async_computation.3 | async-start | bytes 7077888 | tf_op jit(solution)/shard_map/psum | solution.py:15
  115.8 136.1 %all-gather.4.cloned.1.call-start = ((), (), s32[]{:S(2)}) async-start(), calls=%async_computation | async-start | bytes 3538944 | tf_op jit(solution)/shard_map/all_gather | solution.py:55
  189.2 294.5 %all-gather.8.cloned.1.call-start = ((), (), s32[]{:S(2)}) async-start(), calls=%async_computation.2 | async-start | bytes 2359296 | tf_op jit(solution)/shard_map/all_gather | solution.py:67
  252.0 2.8 copy-start
  269.1 1.0 copy-start.5
  423.2 10.6 %copy-start.6 = (f32[128,512]{1,0:T(8,128)}, f32[128,512]{1,0:T(8,128)S(1)}, u32[]{:S(2)}) copy-start(f32[128,512]{1,0:T(8,128)S(1)} %fusion.55) | copy-start | bytes 786436
  426.6 7.2 %copy-start.7 = (f32[128,512]{1,0:T(8,128)}, f32[128,512]{1,0:T(8,128)S(1)}, u32[]{:S(2)}) copy-start(f32[128,512]{1,0:T(8,128)S(1)} %fusion.53) | copy-start | bytes 786436
  430.5 3.3 copy-start.8
  435.7 3.7 copy-start.3
  450.9 38.1 %copy-start.2 = (f32[512,512]{1,0:T(8,128)S(1)}, f32[512,512]{1,0:T(8,128)}, u32[]{:S(2)}) copy-start(f32[512,512]{1,0:T(8,128)} %get-tuple-element.21) | copy-start | bytes 3145732
  483.8 5.3 %copy-start.1 = (f32[1024,512]{1,0:T(8,128)S(1)}, f32[1024,512]{1,0:T(8,128)}, u32[]{:S(2)}) copy-start(f32[1024,512]{1,0:T(8,128)} %all-gather.8.cloned.1.call-done) | copy-start | bytes 6291460
  489.0 2.6 copy-start.4
Sparse Core Ops, SparseCore 0:
  10.2 101.7 all-gather.5
  116.0 73.1 all-reduce.4
  191.4 60.5 all-gather.3
  435.8 47.9 all-gather.7
where the time goes:
time: 523 us; the launch traced here: 513 us
  waiting for transfers between devices  268 us (51%)
  other arithmetic  143 us (27%)
  matrix products  60.3 us (12%)
  local copies, waits for them, and re-layouts  23.9 us (5%)
  between operations  16.9 us (3%)
    all_gather x1, waiting for transfers between devices, on_device(): row_feat = lax.all_gather(features, 'col', axis=1, tiled=True)  102 us
    another operation x14, other arithmetic, on_device(): chol_factor = jnp.linalg.cholesky(corner)  80.7 us
    psum x1, waiting for transfers between devices, spread(): return lax.psum(kept, axis)  73.3 us
    all_gather x1, waiting for transfers between devices, on_device(): head_rows = lax.all_gather(head_part, 'col', axis=1, tiled=True)  59.4 us
    another operation x3, other arithmetic, on_device(): lax.linalg.triangular_solve(chol_factor, jnp.eye(panel_width, dtype=jnp.f...  43.7 us
    all_gather x1, waiting for transfers between devices, on_device(): solved_rows = lax.all_gather(piece_solved, 'col', axis=0, tiled=True)  32.8 us
    dot_general x4, matrix products, gauss_tile(): jnp.dot(left_rows, right_rows.T, precision=lax.Precision.HIGHEST, preferr...  30.9 us
    another operation x12, local copies, waits for them, and re-layouts  13.3 us
  transfers between devices with their start and end apart: 4, of which 4 were waited for; matrix products, arithmetic and copies ran while one was open for 4% of the time, Pallas kernels for 0%

commit v1 on v0

--- a/solution.py
+++ b/solution.py
@@ -1,6 +1,10 @@
+import functools
+
 import jax
 import jax.numpy as jnp
 from jax import lax
+from jax.experimental import pallas as pl
+from jax.experimental.pallas import tpu as pltpu
 from jax.sharding import PartitionSpec as P
 
 D = 1536
@@ -8,6 +12,9 @@
 
 gamma_scale = 0.6
 ridge_value = 0.05
+
+LANES = 128
+GROUP = 8
 
 
 def spread(value, axis, source):
@@ -15,11 +22,11 @@
     return lax.psum(kept, axis)
 
 
-def gauss_tile(left_rows, right_rows, row_start, col_start):
+def gauss_tile(left_rows, right_rows, row_start, col_start, precision=lax.Precision.HIGH):
     left_sq = jnp.sum(left_rows * left_rows, axis=1)
     right_sq = jnp.sum(right_rows * right_rows, axis=1)
     inner_prod = jnp.dot(
-        left_rows, right_rows.T, precision=lax.Precision.HIGHEST, preferred_element_type=jnp.float32
+        left_rows, right_rows.T, precision=precision, preferred_element_type=jnp.float32
     )
     distance = left_sq[:, None] + right_sq[None, :] - 2.0 * inner_prod
     kernel_value = jnp.exp(-distance * (gamma_scale / D))
@@ -33,8 +40,125 @@
 def solve_rows(some_rows, head_rows, first_index, inverse):
     side_tile = gauss_tile(some_rows, head_rows, first_index, 0)
     return jnp.dot(
-        side_tile, inverse.T, precision=lax.Precision.HIGHEST, preferred_element_type=jnp.float32
-    )
+        side_tile, inverse.T, precision=lax.Precision.HIGH, preferred_element_type=jnp.float32
+    )
+
+
+def split_three(value):
+    high = value.astype(jnp.bfloat16).astype(jnp.float32)
+    rest = value - high
+    middle = rest.astype(jnp.bfloat16).astype(jnp.float32)
+    return high, middle, rest - middle
+
+
+def outer_update(rows_here):
+    high, middle, low = split_three(rows_here)
+    right = jnp.concatenate([high, middle, high, low, high, middle], axis=0).astype(jnp.bfloat16)
+    left = jnp.concatenate(
+        [part[:, :LANES] for part in (high, high, middle, high, low, middle)], axis=0
+    ).astype(jnp.bfloat16)
+    return lax.dot_general(
+        left, right, (((0,), (0,)), ((), ())), preferred_element_type=jnp.float32
+    )
+
+
+def factor_group(block_ref, done_ref, first):
+    left_rows = [block_ref[pl.ds(first + t, 1), pl.ds(0, LANES)] for t in range(GROUP)]
+    right_rows = [block_ref[pl.ds(first + t, 1), pl.ds(LANES, LANES)] for t in range(GROUP)]
+    entry = {}
+    for i in range(GROUP):
+        for t in range(i + 1):
+            entry[i, t] = jnp.broadcast_to(
+                left_rows[i][:, first + t : first + t + 1], (1, LANES)
+            )
+    for t in range(GROUP):
+        scale = lax.rsqrt(entry[t, t])
+        ratio = [None] * GROUP
+        for i in range(t + 1, GROUP):
+            ratio[i] = entry[i, t] * scale
+        for i in range(t + 1, GROUP):
+            for k in range(t + 1, i + 1):
+                entry[i, k] = entry[i, k] - ratio[i] * ratio[k]
+        left_rows[t] = left_rows[t] * scale
+        right_rows[t] = right_rows[t] * scale
+        for i in range(t + 1, GROUP):
+            left_rows[i] = left_rows[i] - ratio[i] * left_rows[t]
+            right_rows[i] = right_rows[i] - ratio[i] * right_rows[t]
+    for t in range(GROUP):
+        done_ref[pl.ds(first + t, 1), pl.ds(0, LANES)] = left_rows[t]
+        done_ref[pl.ds(first + t, 1), pl.ds(LANES, LANES)] = right_rows[t]
+    after = first + GROUP
+    if after < LANES:
+        change = outer_update(done_ref[pl.ds(first, GROUP), :])
+        block_ref[pl.ds(after, LANES - after), :] -= change[after:, :]
+
+
+def factor_kernel(corner_ref, chol_ref, inverse_ref, work, block, done):
+    size = corner_ref.shape[0]
+    work[:, pl.ds(0, size)] = corner_ref[...]
+    work[:, pl.ds(size, size)] = (
+        lax.broadcasted_iota(jnp.int32, (size, size), 0)
+        == lax.broadcasted_iota(jnp.int32, (size, size), 1)
+    ).astype(jnp.float32)
+
+    def step(at, carry):
+        start = pl.multiple_of(at * LANES, LANES)
+        rows = pl.ds(start, LANES)
+        block[:, pl.ds(0, LANES)] = work[rows, rows]
+        block[:, pl.ds(LANES, LANES)] = (
+            lax.broadcasted_iota(jnp.int32, (LANES, LANES), 0)
+            == lax.broadcasted_iota(jnp.int32, (LANES, LANES), 1)
+        ).astype(jnp.float32)
+        for first in range(0, LANES, GROUP):
+            factor_group(block, done, first)
+        solved = jnp.dot(
+            done[:, pl.ds(LANES, LANES)],
+            work[rows, :],
+            precision=lax.Precision.HIGHEST,
+            preferred_element_type=jnp.float32,
+        )
+        upper = solved[:, :size]
+        keep = (
+            start + lax.broadcasted_iota(jnp.int32, (LANES, size), 0)
+            <= lax.broadcasted_iota(jnp.int32, (LANES, size), 1)
+        )
+        chol_ref[:, rows] = jnp.where(keep, upper, 0.0).T
+        inverse_ref[rows, :] = solved[:, size:]
+        for other in range(LANES, size, LANES):
+
+            @pl.when(other > start)
+            def _(other=other):
+                across = chol_ref[pl.ds(other, LANES), rows]
+                work[pl.ds(other, LANES), :] -= jnp.dot(
+                    across,
+                    solved,
+                    precision=lax.Precision.HIGHEST,
+                    preferred_element_type=jnp.float32,
+                )
+
+        return carry
+
+    lax.fori_loop(0, size // LANES, step, 0)
+
+
+def factor(corner):
+    size = corner.shape[0]
+    return pl.pallas_call(
+        factor_kernel,
+        out_shape=[jax.ShapeDtypeStruct((size, size), jnp.float32)] * 2,
+        in_specs=[pl.BlockSpec(memory_space=pltpu.VMEM)],
+        out_specs=[pl.BlockSpec(memory_space=pltpu.VMEM)] * 2,
+        scratch_shapes=[
+            pltpu.VMEM((size, 2 * size), jnp.float32),
+            pltpu.VMEM((LANES, 2 * LANES), jnp.float32),
+            pltpu.VMEM((LANES, 2 * LANES), jnp.float32),
+        ],
+        compiler_params=pltpu.CompilerParams(vmem_limit_bytes=32 * 1024 * 1024),
+        name="factor",
+        cost_estimate=pl.CostEstimate(
+            flops=size * size * size * 4, bytes_accessed=3 * 4 * size * size, transcendentals=size
+        ),
+    )(corner)
 
 
 def on_device(features):
@@ -53,11 +177,8 @@
     )
     head_part = spread(features[:panel_width], "row", 0)
     head_rows = lax.all_gather(head_part, "col", axis=1, tiled=True)
-    corner = gauss_tile(head_rows, head_rows, 0, 0)
-    chol_factor = jnp.linalg.cholesky(corner)
-    inverse = lax.linalg.triangular_solve(
-        chol_factor, jnp.eye(panel_width, dtype=jnp.float32), left_side=True, lower=True
-    )
+    corner = gauss_tile(head_rows, head_rows, 0, 0, lax.Precision.HIGHEST)
+    chol_factor, inverse = factor(corner)
     row_start = row_id * row_height
     col_start = col_id * panel_width
     kernel_tile = gauss_tile(row_feat, col_feat, row_start, col_start)
@@ -75,7 +196,7 @@
     col_positions = col_start + jnp.arange(panel_width, dtype=jnp.int32)
     far_panel = jnp.where(col_positions[:, None] < panel_width, 0.0, far_panel)
     trailing = kernel_tile - jnp.dot(
-        masked, far_panel.T, precision=lax.Precision.HIGHEST, preferred_element_type=jnp.float32
+        masked, far_panel.T, precision=lax.Precision.HIGH, preferred_element_type=jnp.float32
     )
     return (panel_out, trailing)
 

time: 523 us -> 361 us (0.69)
  the two profiles are of different devices: /device:TPU:0 before, /device:TPU:31 now
where the time goes in v1:
time: 361 us; the launch traced here: 357 us
  waiting for transfers between devices  272 us (75%)
  Pallas kernels  27.4 us (8%)
  matrix products  25.6 us (7%)
  other arithmetic  14.7 us (4%)
  between operations  13.9 us (4%)
    all_gather x1, waiting for transfers between devices, on_device(): row_feat = lax.all_gather(features, 'col', axis=1, tiled=True)  97.8 us
    psum x1, waiting for transfers between devices, spread(): return lax.psum(kept, axis)  75.3 us
    all_gather x1, waiting for transfers between devices, on_device(): head_rows = lax.all_gather(head_part, 'col', axis=1, tiled=True)  59.8 us
    all_gather x1, waiting for transfers between devices, on_device(): solved_rows = lax.all_gather(piece_solved, 'col', axis=0, tiled=True)  38.2 us
    pallas_call x1, Pallas kernels, factor(): pl.pallas_call(factor_kernel, out_shape=[jax.ShapeDtypeStruct((size, size...  27.4 us
    dot_general x4, matrix products, gauss_tile(): jnp.dot(left_rows, right_rows.T, precision=precision, preferred_element_t...  19.6 us
  transfers between devices with their start and end apart: 4, of which 4 were waited for; matrix products, arithmetic and copies ran while one was open for 3% of the time, Pallas kernels for 0%

profile of v1, /device:TPU:31, one launch (start us, length us, event | category | flops | bytes accessed | tf_op | source)
XLA Modules:
  0.0 356.7 jit_solution(8425529602521493703)
XLA Ops:
  7.2 0.0 all-gather.6.cloned.1.call-start
  7.2 0.7 all-gather.6.cloned.1.call-update
  7.9 0.0 all-reduce.4.cloned.1.call-start
  8.0 1.8 slice_select_fusion
  9.7 97.8 %all-gather.6.cloned.1.call-done = f32[1024,1536]{0,1:T(8,128)} async-done(((f32[1024,192]{0,1:T(8,128)}), f32[1024,1536]{0,1:T(8,128)}) %all-gather.6.cloned.1.call-update) | async-done | bytes 6291472 | tf_op jit(solution)/shard_map/all_gather | solution.py:169
  107.5 3.9 %dynamic-slice_select_fusion = f32[512,1536]{0,1:T(8,128)} fusion(f32[1024,1536]{0,1:T(8,128)} %all-gather.6.cloned.1.call-done, s32[]{:T(128)S(6)} %select_n.69, pred[]{:T(512)S(6)} %eq.67), kind=kLoop, calls=%fused_computation.2 | loop fusion | flops 786432 | bytes 6291461 | tf_op jit(solution)/shard_map/jit(_where)/select_n | solution.py:21
  111.4 0.0 all-reduce.4.cloned.1.call-update
  111.4 0.0 all-gather.4.cloned.1.call-start
  111.5 75.3 %all-reduce.4.cloned.1.call-done = (f32[512,192]{0,1:T(8,128)}, f32[512,1536]{0,1:T(8,128)}) async-done(((f32[512,192]{0,1:T(8,128)}, f32[512,1536]{0,1:T(8,128)}), (f32[512,192]{0,1:T(8,128)}, f32[512,1536]{0,1:T(8,128)})) %all-reduce.4.cloned.1.call-update) | async-done | bytes 3538960 | tf_op jit(solution)/shard_map/psum | solution.py:22
  186.7 0.0 all-gather.4.cloned.1.call-update
  186.8 0.0 all-gather.8.cloned.1.call-start
  186.8 1.4 multiply_reduce_fusion.3
  188.2 59.8 %all-gather.4.cloned.1.call-done = f32[512,1536]{0,1:T(8,128)} async-done(((f32[512,192]{0,1:T(8,128)}), f32[512,1536]{0,1:T(8,128)}) %all-gather.4.cloned.1.call-update) | async-done | bytes 3145744 | tf_op jit(solution)/shard_map/all_gather | solution.py:179
  248.0 0.0 copy-start
  248.0 2.3 multiply_reduce_fusion.2
  250.3 0.5 copy-done
  250.8 5.3 %fusion.16.corner_ref = f32[512,512]{1,0:T(8,128)S(1)} fusion(f32[512,1536]{0,1:T(8,128)S(1)} %copy-done, f32[512]{0:T(512)S(1)} %multiply_reduce_fusion.2), kind=kOutput, calls=%fused_computation.25 | convolution fusion | flops 4833935360 | bytes 4196352 | tf_op jit(solution)/shard_map/dot_general | solution.py:28
  256.1 27.4 %factor.1 = (f32[512,512]{1,0:T(8,128)S(1)}, f32[512,512]{1,0:T(8,128)S(1)}) custom-call(f32[512,512]{1,0:T(8,128)S(1)} %fusion.16.corner_ref), custom_call_target="tpu_custom_call" | custom-call | flops 536870912 | bytes 3145728 | tf_op jit(solution)/shard_map/factor/pallas_call | solution.py:146
  283.6 2.2 fusion.21
  285.8 1.4 fusion.27
  287.2 0.0 all-gather.8.cloned.1.call-update
  287.2 0.0 copy-start.2
  287.2 3.4 multiply_reduce_fusion
  290.7 0.0 copy-start.1
  290.7 0.3 copy-done.2
  290.9 0.3 multiply_reduce_fusion.1
  291.2 1.4 copy-done.1
  292.6 3.1 fusion.15
  295.7 1.0 convolution_select_fusion
  296.8 38.2 %all-gather.8.cloned.1.call-done = f32[1024,512]{1,0:T(8,128)} async-done(((f32[128,512]{1,0:T(8,128)}), f32[1024,512]{1,0:T(8,128)}) %all-gather.8.cloned.1.call-update) | async-done | bytes 2097168 | tf_op jit(solution)/shard_map/all_gather | solution.py:188
  335.0 0.0 copy-start.4
  335.0 3.6 %fusion.5 = f32[1024,512]{1,0:T(8,128)S(1)} fusion(f32[512,512]{1,0:T(8,128)S(1)} %convolution_select_fusion, f32[1024,512]{1,0:T(8,128)} %all-gather.8.cloned.1.call-done, pred[1024]{0:T(1024)(128)(4,1)S(1)} %broadcast_compare_fusion), kind=kOutput, calls=%fused_computation.10 | convolution fusion | flops 1611137024 | bytes 5243904 | tf_op jit(solution)/shard_map/dot_general | solution.py:198
  338.6 0.0 copy-start.3
  338.6 0.0 copy-done.4
  338.6 1.6 pad_select_fusion
  340.2 1.0 copy-done.3
  341.3 8.9 %fusion.4 = f32[1024,512]{1,0:T(8,128)} fusion(f32[1024,512]{1,0:T(8,128)S(1)} %fusion.5, f32[512,1536]{0,1:T(8,128)S(1)} %copy-done.3, f32[1024,1536]{0,1:T(8,128)} %all-gather.6.cloned.1.call-done, s32[512]{0:T(512)S(1)} %iota_add_fusion.1, f32[512]{0:T(512)S(1)} %multiply_reduce_fusion.1, f32[1024]{0:T(1024)S(1)} %multiply_reduce_fusion, ...), kind=kOutput, calls=%fused_computation.9 | convolution fusion | flops 4836556800 | bytes 13643776 | tf_op jit(solution)/shard_map/dot_general | solution.py:28
  (5 shorter events, 0.0 us)
Async XLA Ops:
  7.2 100.4 %all-gather.6.cloned.1.call-start = ((), (), s32[]{:S(2)}) async-start(), calls=%async_computation.1 | async-start | bytes 7077888 | tf_op jit(solution)/shard_map/all_gather | solution.py:169
  7.9 178.9 %all-reduce.4.cloned.1.call-start = ((), (), s32[]{:S(2)}) async-start(), calls=%async_computation.3 | async-start | bytes 7077888 | tf_op jit(solution)/shard_map/psum | solution.py:22
  111.4 136.5 %all-gather.4.cloned.1.call-start = ((), (), s32[]{:S(2)}) async-start(), calls=%async_computation | async-start | bytes 3538944 | tf_op jit(solution)/shard_map/all_gather | solution.py:179
  186.8 148.2 %all-gather.8.cloned.1.call-start = ((), (), s32[]{:S(2)}) async-start(), calls=%async_computation.2 | async-start | bytes 2359296 | tf_op jit(solution)/shard_map/all_gather | solution.py:188
  248.0 2.8 copy-start
  287.2 3.7 %copy-start.2 = (f32[512,1536]{0,1:T(8,128)S(1)}, f32[512,1536]{0,1:T(8,128)}, u32[]{:S(2)}) copy-start(f32[512,1536]{0,1:T(8,128)} %get-tuple-element.7) | copy-start | bytes 9437188
  290.7 2.0 copy-start.1
  335.0 3.6 %copy-start.4 = (f32[1024,512]{1,0:T(8,128)S(1)}, f32[1024,512]{1,0:T(8,128)}, u32[]{:S(2)}) copy-start(f32[1024,512]{1,0:T(8,128)} %all-gather.8.cloned.1.call-done) | copy-start | bytes 6291460
  338.6 2.6 copy-start.3
Sparse Core Ops, SparseCore 0:
  10.2 97.2 all-gather.5
  111.6 75.1 all-reduce.3
  188.9 58.9 all-gather.3
  287.3 47.6 all-gather.7

commit v2 on v1

v2 whole, which is shorter than its diff:
```python
import functools

import jax
import jax.numpy as jnp
from jax import lax
from jax.experimental import pallas as pl
from jax.experimental.pallas import tpu as pltpu
from jax.sharding import PartitionSpec as P

D = 1536


gamma_scale = 0.6
ridge_value = 0.05

MESH = pl.DeviceIdType.MESH
LANES = 128
GROUP = 8


def split_three(value):
    high = value.astype(jnp.bfloat16).astype(jnp.float32)
    rest = value - high
    middle = rest.astype(jnp.bfloat16).astype(jnp.float32)
    return high, middle, rest - middle


def outer_update(rows_here):
    high, middle, low = split_three(rows_here)
    right = jnp.concatenate([high, middle, high, low, high, middle], axis=0).astype(jnp.bfloat16)
    left = jnp.concatenate(
        [part[:, :LANES] for part in (high, high, middle, high, low, middle)], axis=0
    ).astype(jnp.bfloat16)
    return lax.dot_general(
        left, right, (((0,), (0,)), ((), ())), preferred_element_type=jnp.float32
    )


def factor_group(block_ref, done_ref, first):
    left_rows = [block_ref[pl.ds(first + t, 1), pl.ds(0, LANES)] for t in range(GROUP)]
    right_rows = [block_ref[pl.ds(first + t, 1), pl.ds(LANES, LANES)] for t in range(GROUP)]
    entry = {}
    for i in range(GROUP):
        for t in range(i + 1):
            entry[i, t] = jnp.broadcast_to(
                left_rows[i][:, first + t : first + t + 1], (1, LANES)
            )
    for t in range(GROUP):
        scale = lax.rsqrt(entry[t, t])
        scale = scale * (1.5 - 0.5 * entry[t, t] * scale * scale)
        ratio = [None] * GROUP
        for i in range(t + 1, GROUP):
            ratio[i] = entry[i, t] * scale
        for i in range(t + 1, GROUP):
            for k in range(t + 1, i + 1):
                entry[i, k] = entry[i, k] - ratio[i] * ratio[k]
        left_rows[t] = left_rows[t] * scale
        right_rows[t] = right_rows[t] * scale
        for i in range(t + 1, GROUP):
            left_rows[i] = left_rows[i] - ratio[i] * left_rows[t]
            right_rows[i] = right_rows[i] - ratio[i] * right_rows[t]
    for t in range(GROUP):
        done_ref[pl.ds(first + t, 1), pl.ds(0, LANES)] = left_rows[t]
        done_ref[pl.ds(first + t, 1), pl.ds(LANES, LANES)] = right_rows[t]
    after = first + GROUP
    if after < LANES:
        change = outer_update(done_ref[pl.ds(first, GROUP), :])
        block_ref[pl.ds(after, LANES - after), :] -= change[after:, :]


def stacked(value, order, axis):
    parts = split_three(value)
    return jnp.concatenate([parts[at].astype(jnp.bfloat16) for at in order], axis=axis)


FINE = ((0, 0, 1, 0, 2, 1), (0, 1, 0, 2, 0, 1))
PLAIN = ((0, 0, 1), (0, 1, 0))


def product(left, right, axis, orders):
    return lax.dot_general(
        stacked(left, orders[0], axis),
        stacked(right, orders[1], axis),
        (((axis,), (axis,)), ((), ())),
        preferred_element_type=jnp.float32,
    )


def diagonal(rows, columns, offset):
    return (
        offset + lax.broadcasted_iota(jnp.int32, (rows, columns), 0)
        == lax.broadcasted_iota(jnp.int32, (rows, columns), 1)
    )


def gauss_into(out_ref, left, right, offset, orders, step):
    depth, rows = left.shape
    columns = right.shape[1]
    out_ref[...] = jnp.zeros((rows, columns), jnp.float32)

    def add(at, squares):
        span = pl.ds(pl.multiple_of(at * step, step), step)
        one, two = left[span, :], right[span, :]
        out_ref[...] += product(one, two, 0, orders)
        return (
            squares[0] + jnp.sum(one * one, axis=0, keepdims=True),
            squares[1] + jnp.sum(two * two, axis=0, keepdims=True),
        )

    left_sq, right_sq = lax.fori_loop(
        0,
        depth // step,
        add,
        (jnp.zeros((1, rows), jnp.float32), jnp.zeros((1, columns), jnp.float32)),
    )
    left_sq = jnp.broadcast_to(left_sq, (LANES, rows)).T[:, :1]
    distance = left_sq + right_sq - 2.0 * out_ref[...]
    kernel_value = jnp.exp(-distance * (gamma_scale / D))
    out_ref[...] = kernel_value + jnp.where(
        diagonal(rows, columns, offset), ridge_value, 0.0
    )


def factor_into(corner_ref, chol_ref, inverse_ref, work, block, done, beside):
    size = corner_ref.shape[0]
    work[:, pl.ds(0, size)] = corner_ref[...]
    work[:, pl.ds(size, size)] = diagonal(size, size, 0).astype(jnp.float32)

    def step(at, carry):
        start = pl.multiple_of(at * LANES, LANES)
        rows = pl.ds(start, LANES)
        block[:, pl.ds(0, LANES)] = work[rows, rows]
        block[:, pl.ds(LANES, LANES)] = diagonal(LANES, LANES, 0).astype(jnp.float32)
        for first in range(0, LANES, GROUP):
            factor_group(block, done, first)
        solved = jnp.dot(
            done[:, pl.ds(LANES, LANES)],
            work[rows, :],
            precision=lax.Precision.HIGHEST,
            preferred_element_type=jnp.float32,
        )
        upper = solved[:, :size]
        keep = (
            start + lax.broadcasted_iota(jnp.int32, (LANES, size), 0)
            <= lax.broadcasted_iota(jnp.int32, (LANES, size), 1)
        )
        chol_ref[:, rows] = jnp.where(keep, upper, 0.0).T
        inverse_ref[rows, :] = solved[:, size:]
        for other in range(LANES, size, LANES):

            @pl.when(other > start)
            def _(other=other):
                across = chol_ref[pl.ds(other, LANES), rows]
                work[pl.ds(other, LANES), :] -= jnp.dot(
                    across,
                    solved,
                    precision=lax.Precision.HIGHEST,
                    preferred_element_type=jnp.float32,
                )

        beside(at)
        return carry

    lax.fori_loop(0, size // LANES, step, 0)


def panel_kernel(row_count, col_count, own_ref, panel_ref, trail_ref, rows_ref, head_ref, column_ref,
                 corner, chol, inverse, far, side_tile, tile, work, block, done,
                 row_sem, head_sem, col_sem, up_sem, down_sem, side_sem, head_send, col_up, col_down):
    halves, width, centers = own_ref.shape
    row = lax.axis_index("row")
    col = lax.axis_index("col")
    lines = col_count // 2
    line, side = col // 2, col % 2
    owner = col // halves
    part = col % halves

    def copy_of(source, target, send_sem, recv_sem, to_row, to_col):
        return pltpu.make_async_remote_copy(
            src_ref=source,
            dst_ref=target,
            send_sem=send_sem,
            recv_sem=recv_sem,
            device_id=(to_row, to_col),
            device_id_type=MESH,
        )

    def arrived(cond, target, recv_sem):
        pl.when(cond)(lambda: copy_of(target, target, recv_sem, recv_sem, row, col).wait_recv())

    def send(cond, source, target, send_sem, recv_sem, to_row, to_col):
        pl.when(cond)(lambda: copy_of(source, target, send_sem, recv_sem, to_row, to_col).start())

    def slot(half, chunk):
        return rows_ref.at[half, pl.ds(pl.multiple_of(chunk * width, 8), width), :]

    def piece(ref, chunk):
        return ref.at[pl.ds(pl.multiple_of(chunk * width, 8), width), :]

    neighbours = (
        (line < lines - 1, row, col + 2),
        (line > 0, row, col - 2),
        (row >= 0, row, line * 2 + 1 - side),
        (row < row_count - 1, row + 1, col),
        (row > 0, row - 1, col),
    )
    barrier = pltpu.get_barrier_semaphore()
    for cond, to_row, to_col in neighbours:
        pl.when(cond)(
            lambda to_row=to_row, to_col=to_col: pl.semaphore_signal(
                barrier, inc=1, device_id=(to_row, to_col), device_id_type=MESH
            )
        )
    pl.semaphore_wait(barrier, sum(cond.astype(jnp.int32) for cond, _, _ in neighbours))

    def go_up(half, chunk, source, cond):
        send(cond & (line < lines - 1), source, slot(half, chunk), up_sem.at[half, chunk],
             row_sem.at[half, chunk], row, col + 2)

    def go_down(half, chunk, source, cond):
        send(cond & (line > 0), source, slot(half, chunk), down_sem.at[half, chunk],
             row_sem.at[half, chunk], row, col - 2)

    def go_side(half, chunk, source, cond):
        send(cond, source, slot(half, chunk), side_sem.at[half, chunk],
             row_sem.at[half, chunk], row, line * 2 + 1 - side)

    def pass_on(half, chunk, source, cond):
        if half == 0:
            send(cond & (row == 0), source, piece(head_ref, chunk), head_send.at[chunk],
                 head_sem.at[chunk], row + 1, col)
        mine = cond & (row == owner) & (part == half)
        send(mine & (row < row_count - 1), source, piece(column_ref, chunk), col_up.at[chunk],
             col_sem.at[chunk], row + 1, col)
        send(mine & (row > 0), source, piece(column_ref, chunk), col_down.at[chunk],
             col_sem.at[chunk], row - 1, col)

    always = row >= 0
    for half in range(halves):
        own = own_ref.at[half]
        go_side(half, col, own, always)
        go_up(half, col, own, always)
        go_down(half, col, own, always)
        pass_on(half, col, own, always)
    for half in range(halves):
        rows_ref[half, pl.ds(pl.multiple_of(col * width, 8), width), :] = own_ref[half]

    order = [(0, line, always)]
    for away in range(1, lines):
        order.append((away, jnp.maximum(line - away, 0), line >= away))
        order.append((-away, jnp.minimum(line + away, lines - 1), line + away < lines))

    def row_event(half, away, at, cond):
        chunk = at * 2 + side
        if away != 0:
            arrived(cond, slot(half, chunk), row_sem.at[half, chunk])
            (go_up if away > 0 else go_down)(half, chunk, slot(half, chunk), cond)
            go_side(half, chunk, slot(half, chunk), cond)
            pass_on(half, chunk, slot(half, chunk), cond)
        chunk = at * 2 + 1 - side
        arrived(cond, slot(half, chunk), row_sem.at[half, chunk])
        pass_on(half, chunk, slot(half, chunk), cond)

    def head_event(at, cond):
        for chunk in (at * 2 + side, at * 2 + 1 - side):
            taken = cond & (row > 0)
            arrived(taken, piece(head_ref, chunk), head_sem.at[chunk])
            send(taken & (row < row_count - 1), piece(head_ref, chunk), piece(head_ref, chunk),
                 head_send.at[chunk], head_sem.at[chunk], row + 1, col)

    def col_event(at, cond):
        for chunk in (at * 2 + side, at * 2 + 1 - side):
            arrived(cond & (row != owner), piece(column_ref, chunk), col_sem.at[chunk])
            send(cond & (row > owner) & (row < row_count - 1), piece(column_ref, chunk),
                 piece(column_ref, chunk), col_up.at[chunk], col_sem.at[chunk], row + 1, col)
            send(cond & (row < owner) & (row > 0), piece(column_ref, chunk),
                 piece(column_ref, chunk), col_down.at[chunk], col_sem.at[chunk], row - 1, col)

    for away, at, cond in order:
        row_event(0, away, at, cond)
    for away, at, cond in order:
        head_event(at, cond)

    @pl.when(row == 0)
    def _():
        head_ref[...] = rows_ref[0]

    events = [
        functools.partial(row_event, half, away, at, cond)
        for half in range(1, halves)
        for away, at, cond in order
    ] + [functools.partial(col_event, at, cond) for _, at, cond in order]
    turns = centers // LANES

    def beside(turn):
        for number in range(turns):

            @pl.when(turn == number)
            def _(number=number):
                for event in events[
                    len(events) * number // turns : len(events) * (number + 1) // turns
                ]:
                    event()

    step = 2 * LANES if head_ref.shape[0] % (2 * LANES) == 0 else LANES
    gauss_into(corner, head_ref, head_ref, 0, FINE, step)
    factor_into(corner, chol, inverse, work, block, done, beside)

    @pl.when(row == owner)
    def _():
        column_ref[...] = rows_ref[part]

    col_start = col * centers
    gauss_into(side_tile, column_ref, head_ref, col_start, PLAIN, step)
    far[...] = jnp.where(col == 0, 0.0, product(side_tile[...], inverse[...], 1, FINE))

    def finish(half, carry):
        first = (row * halves + half) * centers
        here = pl.ds(pl.multiple_of(half * centers, centers), centers)
        gauss_into(side_tile, rows_ref.at[half], head_ref, first, PLAIN, step)
        solved = product(side_tile[...], inverse[...], 1, FINE)
        top = first == 0
        panel_ref[here, :] = jnp.where(top, chol[...], solved)
        gauss_into(tile, rows_ref.at[half], column_ref, first - col_start, PLAIN, step)
        trail_ref[here, :] = tile[...] - product(
            jnp.where(top, 0.0, solved), far[...], 1, PLAIN
        )
        return carry

    lax.fori_loop(0, halves, finish, 0)

    def gone(cond, source, send_sem):
        pl.when(cond)(lambda: copy_of(source, source, send_sem, send_sem, row, col).wait_send())

    for away, at, cond in order:
        chunk = at * 2 + side
        for half in range(halves):
            gone(cond & (line < lines - 1) & (at <= line), slot(half, chunk), up_sem.at[half, chunk])
            gone(cond & (line > 0) & (at >= line), slot(half, chunk), down_sem.at[half, chunk])
            gone(cond, slot(half, chunk), side_sem.at[half, chunk])
        for chunk in (at * 2 + side, at * 2 + 1 - side):
            gone(cond & (row < row_count - 1), piece(head_ref, chunk), head_send.at[chunk])
            gone(cond & (row >= owner) & (row < row_count - 1), piece(column_ref, chunk), col_up.at[chunk])
            gone(cond & (row <= owner) & (row > 0), piece(column_ref, chunk), col_down.at[chunk])


def factor_panel(turned, row_count, col_count):
    halves, width, centers = turned.shape
    depth = width * col_count
    dma = pltpu.SemaphoreType.DMA
    square = pltpu.VMEM((centers, centers), jnp.float32)
    return pl.pallas_call(
        functools.partial(panel_kernel, row_count, col_count),
        out_shape=[jax.ShapeDtypeStruct((halves * centers, centers), jnp.float32)] * 2,
        in_specs=[pl.BlockSpec(memory_space=pltpu.VMEM)],
        out_specs=[pl.BlockSpec(memory_space=pltpu.VMEM)] * 2,
        scratch_shapes=[
            pltpu.VMEM((halves, depth, centers), jnp.float32),
            pltpu.VMEM((depth, centers), jnp.float32),
            pltpu.VMEM((depth, centers), jnp.float32),
            square,
            square,
            square,
            square,
            square,
            square,
            pltpu.VMEM((centers, 2 * centers), jnp.float32),
            pltpu.VMEM((LANES, 2 * LANES), jnp.float32),
            pltpu.VMEM((LANES, 2 * LANES), jnp.float32),
            dma((halves, col_count)),
            dma((col_count,)),
            dma((col_count,)),
            dma((halves, col_count)),
            dma((halves, col_count)),
            dma((halves, col_count)),
            dma((col_count,)),
            dma((col_count,)),
            dma((col_count,)),
        ],
        compiler_params=pltpu.CompilerParams(
            collective_id=0, has_side_effects=True, vmem_limit_bytes=56 * 1024 * 1024
        ),
        name="panel",
    )(turned)


def on_device(features):
    row_count = lax.axis_size("row")
    col_count = lax.axis_size("col")
    row_height, width = features.shape
    halves = col_count // row_count
    turned = features.reshape(halves, row_height // halves, width).transpose(0, 2, 1)
    return tuple(factor_panel(turned, row_count, col_count))


def solution(mesh):
    return jax.shard_map(
        on_device,
        mesh=mesh,
        in_specs=(P("row", "col"),),
        out_specs=(P("row", None), P("row", "col")),
        check_vma=False,
    )
```

time: 361 us -> 228 us (0.63)
  the two profiles are of different devices: /device:TPU:31 before, /device:TPU:26 now
where the time goes in v2:
time: 228 us
  Pallas kernels  221 us (97%)
  local copies, waits for them, and re-layouts  6.62 us (3%)
    pallas_call x1, Pallas kernels, factor_panel(): pl.pallas_call(functools.partial(panel_kernel, row_count, col_count), out...  221 us

profile of v2, /device:TPU:26, one launch (start us, length us, event | category | flops | bytes accessed | tf_op | source)
XLA Modules:
  0.0 228.1 jit_solution(10583917913299152721)
XLA Ops:
  0.6 2.1 copy.6
  2.7 220.8 %panel.1 = (f32[1024,512]{1,0:T(8,128)}, f32[1024,512]{1,0:T(8,128)}) custom-call(f32[2,192,512]{2,1,0:T(8,128)} %bitcast.7), custom_call_target="tpu_custom_call" | custom-call | tf_op jit(solution)/shard_map/panel/pallas_call | solution.py:352
  223.5 0.0 copy-start
  223.5 3.2 %copy.9 = f32[1024,512]{1,0:T(8,128)} copy(f32[1024,512]{1,0:T(8,128)} %get-tuple-element.4) | data formatting | bytes 4194304
  226.7 0.0 copy-done
  226.7 1.3 copy.10
Async XLA Ops:
  223.5 3.2 %copy-start = (f32[1024,512]{1,0:T(8,128)S(1)}, f32[1024,512]{1,0:T(8,128)}, u32[]{:S(2)}) copy-start(f32[1024,512]{1,0:T(8,128)} %get-tuple-element.5) | copy-start | bytes 6291460

commit v3 on v2

--- a/solution.py
+++ b/solution.py
@@ -93,7 +93,7 @@
     )
 
 
-def gauss_into(out_ref, left, right, offset, orders, step):
+def gauss_into(out_ref, left, right, offset, orders, step, beside=None):
     depth, rows = left.shape
     columns = right.shape[1]
     out_ref[...] = jnp.zeros((rows, columns), jnp.float32)
@@ -102,6 +102,8 @@
         span = pl.ds(pl.multiple_of(at * step, step), step)
         one, two = left[span, :], right[span, :]
         out_ref[...] += product(one, two, 0, orders)
+        if beside is not None:
+            beside(at)
         return (
             squares[0] + jnp.sum(one * one, axis=0, keepdims=True),
             squares[1] + jnp.sum(two * two, axis=0, keepdims=True),
@@ -165,7 +167,7 @@
 
 
 def panel_kernel(row_count, col_count, own_ref, panel_ref, trail_ref, rows_ref, head_ref, column_ref,
-                 corner, chol, inverse, far, side_tile, tile, work, block, done,
+                 corner, chol, inverse, far, side_tiles, work, block, done, inverse_sem,
                  row_sem, head_sem, col_sem, up_sem, down_sem, side_sem, head_send, col_up, col_down):
     halves, width, centers = own_ref.shape
     row = lax.axis_index("row")
@@ -278,60 +280,93 @@
 
     for away, at, cond in order:
         row_event(0, away, at, cond)
-    for away, at, cond in order:
-        head_event(at, cond)
+    rest = [
+        functools.partial(row_event, half, away, at, cond)
+        for half in range(1, halves)
+        for away, at, cond in order
+    ]
+    heads = [functools.partial(head_event, at, cond) for _, at, cond in order]
+    columns = [functools.partial(col_event, at, cond) for _, at, cond in order]
+
+    def among(events, turns):
+        def beside(turn):
+            for number in range(turns):
+
+                @pl.when(turn == number)
+                def _(number=number):
+                    for event in events[
+                        len(events) * number // turns : len(events) * (number + 1) // turns
+                    ]:
+                        event()
+
+        return beside
+
+    depth = head_ref.shape[0]
+    step = 2 * LANES if depth % (2 * LANES) == 0 else LANES
+    col_start = col * centers
+    first_row = row * halves * centers
+
+    def send_inverse(cond):
+        send(cond & (row < row_count - 1), inverse, inverse, inverse_sem.at[0], inverse_sem.at[1],
+             row + 1, col)
 
     @pl.when(row == 0)
     def _():
         head_ref[...] = rows_ref[0]
-
-    events = [
-        functools.partial(row_event, half, away, at, cond)
-        for half in range(1, halves)
-        for away, at, cond in order
-    ] + [functools.partial(col_event, at, cond) for _, at, cond in order]
-    turns = centers // LANES
-
-    def beside(turn):
-        for number in range(turns):
-
-            @pl.when(turn == number)
-            def _(number=number):
-                for event in events[
-                    len(events) * number // turns : len(events) * (number + 1) // turns
-                ]:
-                    event()
-
-    step = 2 * LANES if head_ref.shape[0] % (2 * LANES) == 0 else LANES
-    gauss_into(corner, head_ref, head_ref, 0, FINE, step)
-    factor_into(corner, chol, inverse, work, block, done, beside)
+        gauss_into(corner, head_ref, head_ref, 0, FINE, step)
+        factor_into(corner, chol, inverse, work, block, done, among(rest + columns, centers // LANES))
+        send_inverse(always)
+
+    @pl.when(row > 0)
+    def _():
+        for number, event in enumerate(rest):
+            event()
+            if number < len(heads):
+                heads[number]()
+        for event in heads[len(rest):]:
+            event()
+        gauss_into(side_tiles.at[0], rows_ref.at[0], head_ref, first_row, PLAIN, step,
+                   among(columns, depth // step))
 
     @pl.when(row == owner)
     def _():
         column_ref[...] = rows_ref[part]
 
-    col_start = col * centers
-    gauss_into(side_tile, column_ref, head_ref, col_start, PLAIN, step)
-    far[...] = jnp.where(col == 0, 0.0, product(side_tile[...], inverse[...], 1, FINE))
+    def side_of(half, carry):
+        gauss_into(side_tiles.at[half], rows_ref.at[half], head_ref, first_row + half * centers, PLAIN, step)
+        return carry
+
+    def tile_of(half, carry):
+        here = pl.ds(pl.multiple_of(half * centers, centers), centers)
+        gauss_into(trail_ref.at[here, :], rows_ref.at[half], column_ref,
+                   first_row + half * centers - col_start, PLAIN, step)
+        return carry
+
+    lax.fori_loop(1, halves, side_of, 0)
+    lax.fori_loop(0, halves, tile_of, 0)
+    gauss_into(far, column_ref, head_ref, col_start, PLAIN, step)
+
+    arrived(row > 0, inverse, inverse_sem.at[1])
+    send_inverse(row > 0)
+    far[...] = jnp.where(col == 0, 0.0, product(far[...], inverse[...], 1, FINE))
 
     def finish(half, carry):
-        first = (row * halves + half) * centers
         here = pl.ds(pl.multiple_of(half * centers, centers), centers)
-        gauss_into(side_tile, rows_ref.at[half], head_ref, first, PLAIN, step)
-        solved = product(side_tile[...], inverse[...], 1, FINE)
-        top = first == 0
-        panel_ref[here, :] = jnp.where(top, chol[...], solved)
-        gauss_into(tile, rows_ref.at[half], column_ref, first - col_start, PLAIN, step)
-        trail_ref[here, :] = tile[...] - product(
-            jnp.where(top, 0.0, solved), far[...], 1, PLAIN
-        )
+        solved = product(side_tiles[half], inverse[...], 1, FINE)
+        panel_ref[here, :] = solved
+        trail_ref[here, :] -= product(solved, far[...], 1, PLAIN)
         return carry
 
-    lax.fori_loop(0, halves, finish, 0)
+    lax.fori_loop(jnp.where(row == 0, 1, 0), halves, finish, 0)
+
+    @pl.when(row == 0)
+    def _():
+        panel_ref[pl.ds(0, centers), :] = chol[...]
 
     def gone(cond, source, send_sem):
         pl.when(cond)(lambda: copy_of(source, source, send_sem, send_sem, row, col).wait_send())
 
+    gone(row < row_count - 1, inverse, inverse_sem.at[0])
     for away, at, cond in order:
         chunk = at * 2 + side
         for half in range(halves):
@@ -362,11 +397,11 @@
             square,
             square,
             square,
-            square,
-            square,
+            pltpu.VMEM((halves, centers, centers), jnp.float32),
             pltpu.VMEM((centers, 2 * centers), jnp.float32),
             pltpu.VMEM((LANES, 2 * LANES), jnp.float32),
             pltpu.VMEM((LANES, 2 * LANES), jnp.float32),
+            dma((2,)),
             dma((halves, col_count)),
             dma((col_count,)),
             dma((col_count,)),

time: 228 us -> 183 us (0.80)
  the two profiles are of different devices: /device:TPU:26 before, /device:TPU:31 now
where the time goes in v3:
time: 183 us
  Pallas kernels  175 us (96%)
  local copies, waits for them, and re-layouts  6.62 us (4%)
    pallas_call x1, Pallas kernels, factor_panel(): pl.pallas_call(functools.partial(panel_kernel, row_count, col_count), out...  175 us
    unnamed x4, local copies, waits for them, and re-layouts  4.55 us

profile of v3, /device:TPU:31, one launch (start us, length us, event | category | flops | bytes accessed | tf_op | source)
XLA Modules:
  0.0 182.5 jit_solution(2537032359481192218)
XLA Ops:
  0.6 2.1 %copy.6 = f32[24,2,8,512]{3,2,0,1:T(8,128)} copy(f32[24,2,8,512]{3,2,1,0:T(8,128)} %bitcast.8) | data formatting | bytes 1572864 | tf_op jit(solution)/shard_map/reshape | solution.py:427
  2.7 175.3 %panel.1 = (f32[1024,512]{1,0:T(8,128)}, f32[1024,512]{1,0:T(8,128)}) custom-call(f32[2,192,512]{2,1,0:T(8,128)} %bitcast.7), custom_call_target="tpu_custom_call" | custom-call | tf_op jit(solution)/shard_map/panel/pallas_call | solution.py:387
  178.0 0.0 copy-start
  178.0 3.2 %copy.9 = f32[1024,512]{1,0:T(8,128)} copy(f32[1024,512]{1,0:T(8,128)} %get-tuple-element.4) | data formatting | bytes 4194304
  181.2 0.0 copy-done
  181.2 1.3 copy.10
Async XLA Ops:
  178.0 3.2 %copy-start = (f32[1024,512]{1,0:T(8,128)S(1)}, f32[1024,512]{1,0:T(8,128)}, u32[]{:S(2)}) copy-start(f32[1024,512]{1,0:T(8,128)} %get-tuple-element.5) | copy-start | bytes 6291460

commit v4 on v3

--- a/solution.py
+++ b/solution.py
@@ -238,12 +238,15 @@
              col_sem.at[chunk], row - 1, col)
 
     always = row >= 0
-    for half in range(halves):
+
+    def own_sends(half):
         own = own_ref.at[half]
         go_side(half, col, own, always)
         go_up(half, col, own, always)
         go_down(half, col, own, always)
         pass_on(half, col, own, always)
+
+    own_sends(0)
     for half in range(halves):
         rows_ref[half, pl.ds(pl.multiple_of(col * width, 8), width), :] = own_ref[half]
 
@@ -278,8 +281,11 @@
             send(cond & (row < owner) & (row > 0), piece(column_ref, chunk),
                  piece(column_ref, chunk), col_down.at[chunk], col_sem.at[chunk], row - 1, col)
 
-    for away, at, cond in order:
+    for number, (away, at, cond) in enumerate(order):
         row_event(0, away, at, cond)
+        if number == min(2, len(order) - 1):
+            for half in range(1, halves):
+                own_sends(half)
     rest = [
         functools.partial(row_event, half, away, at, cond)
         for half in range(1, halves)
@@ -314,18 +320,23 @@
     def _():
         head_ref[...] = rows_ref[0]
         gauss_into(corner, head_ref, head_ref, 0, FINE, step)
-        factor_into(corner, chol, inverse, work, block, done, among(rest + columns, centers // LANES))
+        slots = centers // LANES
+        late = [lambda: None] * (len(rest) // (slots - 1))
+        factor_into(corner, chol, inverse, work, block, done, among(late + rest, slots))
         send_inverse(always)
 
     @pl.when(row > 0)
     def _():
-        for number, event in enumerate(rest):
-            event()
-            if number < len(heads):
-                heads[number]()
-        for event in heads[len(rest):]:
+        for event in heads:
             event()
         gauss_into(side_tiles.at[0], rows_ref.at[0], head_ref, first_row, PLAIN, step,
+                   among(rest, depth // step))
+
+    if halves == 1:
+        for event in columns:
+            event()
+    else:
+        gauss_into(side_tiles.at[1], rows_ref.at[1], head_ref, first_row + centers, PLAIN, step,
                    among(columns, depth // step))
 
     @pl.when(row == owner)
@@ -342,7 +353,7 @@
                    first_row + half * centers - col_start, PLAIN, step)
         return carry
 
-    lax.fori_loop(1, halves, side_of, 0)
+    lax.fori_loop(2, halves, side_of, 0)
     lax.fori_loop(0, halves, tile_of, 0)
     gauss_into(far, column_ref, head_ref, col_start, PLAIN, step)
 

time: 183 us -> 210 us (1.15)
  Pallas kernels: 175 us -> 203 us
    pallas_call x1, Pallas kernels: 175 us -> 203 us  [factor_panel(): pl.pallas_call(functools.partial(panel_kernel, row_count, col_count), out...]
where the time goes in v4:
time: 210 us
  Pallas kernels  203 us (97%)
  local copies, waits for them, and re-layouts  6.62 us (3%)
    pallas_call x1, Pallas kernels, factor_panel(): pl.pallas_call(functools.partial(panel_kernel, row_count, col_count), out...  203 us
    unnamed x4, local copies, waits for them, and re-layouts  4.55 us

profile of v4, /device:TPU:31, one launch (start us, length us, event | category | flops | bytes accessed | tf_op | source)
XLA Modules:
  0.0 210.0 jit_solution(1880527088092967881)
XLA Ops:
  0.6 2.1 copy.6
  2.7 202.7 %panel.1 = (f32[1024,512]{1,0:T(8,128)}, f32[1024,512]{1,0:T(8,128)}) custom-call(f32[2,192,512]{2,1,0:T(8,128)} %bitcast.7), custom_call_target="tpu_custom_call" | custom-call | tf_op jit(solution)/shard_map/panel/pallas_call | solution.py:398
  205.4 0.0 copy-start
  205.4 3.2 %copy.9 = f32[1024,512]{1,0:T(8,128)} copy(f32[1024,512]{1,0:T(8,128)} %get-tuple-element.4) | data formatting | bytes 4194304
  208.7 0.0 copy-done
  208.7 1.3 copy.10
Async XLA Ops:
  205.4 3.2 %copy-start = (f32[1024,512]{1,0:T(8,128)S(1)}, f32[1024,512]{1,0:T(8,128)}, u32[]{:S(2)}) copy-start(f32[1024,512]{1,0:T(8,128)} %get-tuple-element.5) | copy-start | bytes 6291460

commit v5 on v3

--- a/solution.py
+++ b/solution.py
@@ -168,7 +168,8 @@
 
 def panel_kernel(row_count, col_count, own_ref, panel_ref, trail_ref, rows_ref, head_ref, column_ref,
                  corner, chol, inverse, far, side_tiles, work, block, done, inverse_sem,
-                 row_sem, head_sem, col_sem, up_sem, down_sem, side_sem, head_send, col_up, col_down):
+                 row_sem, head_sem, col_sem, up_sem, down_sem, side_sem, head_up, head_mate,
+                 col_up, col_down, col_mate):
     halves, width, centers = own_ref.shape
     row = lax.axis_index("row")
     col = lax.axis_index("col")
@@ -176,6 +177,7 @@
     line, side = col // 2, col % 2
     owner = col // halves
     part = col % halves
+    mate = row + 1 - row % 2 * 2
 
     def copy_of(source, target, send_sem, recv_sem, to_row, to_col):
         return pltpu.make_async_remote_copy(
@@ -203,8 +205,9 @@
         (line < lines - 1, row, col + 2),
         (line > 0, row, col - 2),
         (row >= 0, row, line * 2 + 1 - side),
-        (row < row_count - 1, row + 1, col),
-        (row > 0, row - 1, col),
+        (row >= 0, mate, col),
+        (row < row_count - 2, row + 2, col),
+        (row > 1, row - 2, col),
     )
     barrier = pltpu.get_barrier_semaphore()
     for cond, to_row, to_col in neighbours:
@@ -227,23 +230,37 @@
         send(cond, source, slot(half, chunk), side_sem.at[half, chunk],
              row_sem.at[half, chunk], row, line * 2 + 1 - side)
 
+    def spread_head(chunk, source, cond):
+        cond = cond & (row % 2 == 0)
+        target = piece(head_ref, chunk)
+        send(cond, source, target, head_mate.at[chunk], head_sem.at[chunk], mate, col)
+        send(cond & (row < row_count - 2), source, target, head_up.at[chunk], head_sem.at[chunk], row + 2, col)
+
+    def spread_column(chunk, source, cond):
+        cond = cond & (row % 2 == owner % 2)
+        target = piece(column_ref, chunk)
+        send(cond & (row >= owner) & (row < row_count - 2), source, target, col_up.at[chunk],
+             col_sem.at[chunk], row + 2, col)
+        send(cond & (row <= owner) & (row > 1), source, target, col_down.at[chunk],
+             col_sem.at[chunk], row - 2, col)
+        send(cond, source, target, col_mate.at[chunk], col_sem.at[chunk], mate, col)
+
     def pass_on(half, chunk, source, cond):
         if half == 0:
-            send(cond & (row == 0), source, piece(head_ref, chunk), head_send.at[chunk],
-                 head_sem.at[chunk], row + 1, col)
-        mine = cond & (row == owner) & (part == half)
-        send(mine & (row < row_count - 1), source, piece(column_ref, chunk), col_up.at[chunk],
-             col_sem.at[chunk], row + 1, col)
-        send(mine & (row > 0), source, piece(column_ref, chunk), col_down.at[chunk],
-             col_sem.at[chunk], row - 1, col)
+            spread_head(chunk, source, cond & (row == 0))
+        spread_column(chunk, source, cond & (row == owner) & (part == half))
 
     always = row >= 0
-    for half in range(halves):
+
+    def own_sends(half):
         own = own_ref.at[half]
         go_side(half, col, own, always)
         go_up(half, col, own, always)
         go_down(half, col, own, always)
         pass_on(half, col, own, always)
+
+    for half in range(halves):
+        own_sends(half)
     for half in range(halves):
         rows_ref[half, pl.ds(pl.multiple_of(col * width, 8), width), :] = own_ref[half]
 
@@ -267,16 +284,13 @@
         for chunk in (at * 2 + side, at * 2 + 1 - side):
             taken = cond & (row > 0)
             arrived(taken, piece(head_ref, chunk), head_sem.at[chunk])
-            send(taken & (row < row_count - 1), piece(head_ref, chunk), piece(head_ref, chunk),
-                 head_send.at[chunk], head_sem.at[chunk], row + 1, col)
+            spread_head(chunk, piece(head_ref, chunk), taken)
 
     def col_event(at, cond):
         for chunk in (at * 2 + side, at * 2 + 1 - side):
-            arrived(cond & (row != owner), piece(column_ref, chunk), col_sem.at[chunk])
-            send(cond & (row > owner) & (row < row_count - 1), piece(column_ref, chunk),
-                 piece(column_ref, chunk), col_up.at[chunk], col_sem.at[chunk], row + 1, col)
-            send(cond & (row < owner) & (row > 0), piece(column_ref, chunk),
-                 piece(column_ref, chunk), col_down.at[chunk], col_sem.at[chunk], row - 1, col)
+            taken = cond & (row != owner)
+            arrived(taken, piece(column_ref, chunk), col_sem.at[chunk])
+            spread_column(chunk, piece(column_ref, chunk), taken)
 
     for away, at, cond in order:
         row_event(0, away, at, cond)
@@ -307,26 +321,36 @@
     first_row = row * halves * centers
 
     def send_inverse(cond):
-        send(cond & (row < row_count - 1), inverse, inverse, inverse_sem.at[0], inverse_sem.at[1],
-             row + 1, col)
+        cond = cond & (row % 2 == 0)
+        send(cond & (row < row_count - 2), inverse, inverse, inverse_sem.at[0], inverse_sem.at[2],
+             row + 2, col)
+        send(cond, inverse, inverse, inverse_sem.at[1], inverse_sem.at[2], mate, col)
 
     @pl.when(row == 0)
     def _():
         head_ref[...] = rows_ref[0]
         gauss_into(corner, head_ref, head_ref, 0, FINE, step)
-        factor_into(corner, chol, inverse, work, block, done, among(rest + columns, centers // LANES))
+        slots = centers // LANES
+        late = [lambda: None] * (len(rest) // (slots - 1))
+        factor_into(corner, chol, inverse, work, block, done, among(late + rest, slots))
         send_inverse(always)
 
     @pl.when(row > 0)
     def _():
-        for number, event in enumerate(rest):
-            event()
-            if number < len(heads):
-                heads[number]()
-        for event in heads[len(rest):]:
-            event()
+        for number in range(max(len(rest), len(heads))):
+            for event in rest[number : number + 1] + heads[number : number + 1]:
+                event()
         gauss_into(side_tiles.at[0], rows_ref.at[0], head_ref, first_row, PLAIN, step,
                    among(columns, depth // step))
+
+    @pl.when(row == 0)
+    def _():
+        if halves == 1:
+            for event in columns:
+                event()
+        else:
+            gauss_into(side_tiles.at[1], rows_ref.at[1], head_ref, first_row + centers, PLAIN, step,
+                       among(columns, depth // step))
 
     @pl.when(row == owner)
     def _():
@@ -342,11 +366,11 @@
                    first_row + half * centers - col_start, PLAIN, step)
         return carry
 
-    lax.fori_loop(1, halves, side_of, 0)
+    lax.fori_loop(jnp.where(row == 0, 2, 1), halves, side_of, 0)
     lax.fori_loop(0, halves, tile_of, 0)
     gauss_into(far, column_ref, head_ref, col_start, PLAIN, step)
 
-    arrived(row > 0, inverse, inverse_sem.at[1])
+    arrived(row > 0, inverse, inverse_sem.at[2])
     send_inverse(row > 0)
     far[...] = jnp.where(col == 0, 0.0, product(far[...], inverse[...], 1, FINE))
 
@@ -366,7 +390,8 @@
     def gone(cond, source, send_sem):
         pl.when(cond)(lambda: copy_of(source, source, send_sem, send_sem, row, col).wait_send())
 
-    gone(row < row_count - 1, inverse, inverse_sem.at[0])
+    gone((row % 2 == 0) & (row < row_count - 2), inverse, inverse_sem.at[0])
+    gone(row % 2 == 0, inverse, inverse_sem.at[1])
     for away, at, cond in order:
         chunk = at * 2 + side
         for half in range(halves):
@@ -374,9 +399,14 @@
             gone(cond & (line > 0) & (at >= line), slot(half, chunk), down_sem.at[half, chunk])
             gone(cond, slot(half, chunk), side_sem.at[half, chunk])
         for chunk in (at * 2 + side, at * 2 + 1 - side):
-            gone(cond & (row < row_count - 1), piece(head_ref, chunk), head_send.at[chunk])
-            gone(cond & (row >= owner) & (row < row_count - 1), piece(column_ref, chunk), col_up.at[chunk])
-            gone(cond & (row <= owner) & (row > 0), piece(column_ref, chunk), col_down.at[chunk])
+            head = piece(head_ref, chunk)
+            gone(cond & (row % 2 == 0) & (row < row_count - 2), head, head_up.at[chunk])
+            gone(cond & (row % 2 == 0), head, head_mate.at[chunk])
+            ours = cond & (row % 2 == owner % 2)
+            column = piece(column_ref, chunk)
+            gone(ours & (row >= owner) & (row < row_count - 2), column, col_up.at[chunk])
+            gone(ours & (row <= owner) & (row > 1), column, col_down.at[chunk])
+            gone(ours, column, col_mate.at[chunk])
 
 
 def factor_panel(turned, row_count, col_count):
@@ -401,13 +431,15 @@
             pltpu.VMEM((centers, 2 * centers), jnp.float32),
             pltpu.VMEM((LANES, 2 * LANES), jnp.float32),
             pltpu.VMEM((LANES, 2 * LANES), jnp.float32),
-            dma((2,)),
+            dma((3,)),
             dma((halves, col_count)),
             dma((col_count,)),
             dma((col_count,)),
             dma((halves, col_count)),
             dma((halves, col_count)),
             dma((halves, col_count)),
+            dma((col_count,)),
+            dma((col_count,)),
             dma((col_count,)),
             dma((col_count,)),
             dma((col_count,)),

time: 183 us -> 160 us (0.87)
  the two profiles are of different devices: /device:TPU:31 before, /device:TPU:7 now
where the time goes in v5:
time: 160 us
  Pallas kernels  153 us (96%)
  local copies, waits for them, and re-layouts  6.62 us (4%)
    pallas_call x1, Pallas kernels, factor_panel(): pl.pallas_call(functools.partial(panel_kernel, row_count, col_count), out...  153 us
    unnamed x4, local copies, waits for them, and re-layouts  4.55 us

profile of v5, /device:TPU:7, one launch (start us, length us, event | category | flops | bytes accessed | tf_op | source)
XLA Modules:
  0.0 160.3 jit_solution(6318590010974411116)
XLA Ops:
  0.6 2.1 %copy.6 = f32[24,2,8,512]{3,2,0,1:T(8,128)} copy(f32[24,2,8,512]{3,2,1,0:T(8,128)} %bitcast.8) | data formatting | bytes 1572864 | tf_op jit(solution)/shard_map/reshape | solution.py:459
  2.7 153.0 %panel.1 = (f32[1024,512]{1,0:T(8,128)}, f32[1024,512]{1,0:T(8,128)}) custom-call(f32[2,192,512]{2,1,0:T(8,128)} %bitcast.7), custom_call_target="tpu_custom_call" | custom-call | tf_op jit(solution)/shard_map/panel/pallas_call | solution.py:417
  155.7 0.0 copy-start
  155.7 3.2 %copy.9 = f32[1024,512]{1,0:T(8,128)} copy(f32[1024,512]{1,0:T(8,128)} %get-tuple-element.4) | data formatting | bytes 4194304
  158.9 0.0 copy-done
  158.9 1.3 copy.10
Async XLA Ops:
  155.7 3.2 %copy-start = (f32[1024,512]{1,0:T(8,128)S(1)}, f32[1024,512]{1,0:T(8,128)}, u32[]{:S(2)}) copy-start(f32[1024,512]{1,0:T(8,128)} %get-tuple-element.5) | copy-start | bytes 6291460
